TPU v7x, 32 devices: a whole 2x2x4 slice. The times are simulated.
32 devices in a mesh: chan: 8 (over y, x, core), tile: 4 (over z).
Axes of the slice: x: 2, y: 2, z: 4, core: 2. Of those that a mesh axis runs over, the one named last changes fastest.
Arguments:
- visibility: float32 [2, 8192], P(None, ('chan', 'tile')), may hold values from -6 to 6
- kernel_table: bfloat16 [2048, 128], replicated, may hold values from -0.8984375 to 0.8984375
- cell_index: int32 [8192], P(('chan', 'tile')), may hold values from 0 to 65535
- tile_index: int32 [8192, 1], P(('chan', 'tile')), may hold values from 0 to 3; in each aligned block of 256 rows (0 to 255, 256 to 511, ...) at most 128 rows name the same one
- plane_index: int32 [8192], P(('chan', 'tile')), may hold values from 0 to 31
- offset_index: int32 [8192], P(('chan', 'tile')), may hold values from 0 to 63
Outputs:
- gridded: float32 [2, 64, 4096], P(None, 'tile', 'chan')
Inputs may be any that keep to these rules, and one draw needn't show every extreme that they name: `tile_index`: among the rows of one device at most 128 name the same tile, and in some device some tile is named by exactly 128 rows.
All inputs are finite; a program needn't handle non-finite values.
Results may differ from a plain program's by a relative error of at most 0.0029.
Values may be sent and summed in bfloat16 or wider, within the bound.
No kernel may reach another device: no remote copies, remote signals or barrier semaphores. Data moves between devices by JAX's collectives and lax.ppermute only.
A program may use at most 64 MiB of HBM per device.

v0:
```python
import jax
import jax.numpy as jnp
from jax import lax
from jax.sharding import PartitionSpec as P

GRID_U = 4096
SUPPORT = 8
OVERSAMPLE = 8
TILE_V = 16
CAPACITY = 128
SUB_V = 24


def passed_along(shard, axis, by):
    size = lax.axis_size(axis)
    pairs = [(i, i + by) for i in range(size) if 0 <= i + by < size]
    return lax.ppermute(shard, axis, pairs)


def weigh(kernel_table, vis_real, vis_imag, kind):
    area = SUPPORT * SUPPORT
    kern = jnp.take(kernel_table, kind, axis=0).astype(jnp.float32)
    real_kern = kern[:, :area]
    imag_kern = kern[:, area:]
    real_part = vis_real[:, None] * real_kern - vis_imag[:, None] * imag_kern
    imag_part = vis_real[:, None] * imag_kern + vis_imag[:, None] * real_kern
    return jnp.concatenate([real_part, imag_part], axis=1).astype(jnp.bfloat16)


def body(visibility, kernel_table, cell_index, tile_index, plane_index, offset_index):
    tiles = lax.axis_size("tile")
    area = SUPPORT * SUPPORT
    slots = tiles * CAPACITY
    destination = tile_index[:, 0]
    marks = (destination[:, None] == jnp.arange(tiles, dtype=jnp.int32)[None, :]).astype(jnp.int32)
    ranks = jnp.sum(jnp.cumsum(marks, axis=0) * marks, axis=1) - 1
    target = destination * CAPACITY + ranks
    kind = plane_index * (OVERSAMPLE * OVERSAMPLE) + offset_index
    weighted = weigh(kernel_table, visibility[0], visibility[1], kind)
    send_values = jnp.zeros((slots, 2 * area), jnp.bfloat16).at[target].set(weighted)
    send_cells = jnp.zeros((slots,), jnp.int32).at[target].set(cell_index)
    arrived, cells = (
        lax.all_to_all(
            send_values.reshape(tiles, CAPACITY, 2 * area),
            "tile",
            split_axis=0,
            concat_axis=0,
            tiled=True,
        ),
        lax.all_to_all(
            send_cells.reshape(tiles, CAPACITY), "tile", split_axis=0, concat_axis=0, tiled=True
        ),
    )
    weighted_all = arrived.reshape(slots, 2 * area)
    cells = cells.reshape(slots)
    row_pos = cells // GRID_U
    col_pos = cells % GRID_U
    taps = jnp.arange(SUPPORT, dtype=jnp.int32)
    placed = (
        row_pos[:, None, None] + taps[None, :, None]
        == jnp.arange(SUB_V, dtype=jnp.int32)[None, None, :]
    ).astype(jnp.bfloat16)
    values = weighted_all.reshape(slots, 2, SUPPORT, SUPPORT)
    spread = jnp.einsum("rjy,rcij->rcyi", placed, values, preferred_element_type=jnp.float32)
    spread = spread.astype(jnp.bfloat16).reshape(slots, 2 * SUB_V * SUPPORT)
    width = min(GRID_U, 1024)
    block = min(slots, 1024)
    padded = jnp.zeros((2, SUB_V, GRID_U + SUPPORT), jnp.float32)
    for first_col in range(0, GRID_U, width):
        section = jnp.zeros((2 * SUB_V * SUPPORT, width), jnp.float32)
        for first_row in range(0, slots, block):
            local = col_pos[first_row : first_row + block] - first_col
            onehot = (local[:, None] == jnp.arange(width, dtype=jnp.int32)[None, :]).astype(
                jnp.bfloat16
            )
            section = section + lax.dot_general(
                spread[first_row : first_row + block],
                onehot,
                (((0,), (0,)), ((), ())),
                preferred_element_type=jnp.float32,
            )
        section = section.reshape(2, SUB_V, SUPPORT, width)
        strip = jnp.zeros((2, SUB_V, width + SUPPORT), jnp.float32)
        for tap in range(SUPPORT):
            strip = strip + jnp.pad(section[:, :, tap, :], ((0, 0), (0, 0), (tap, SUPPORT - tap)))
        padded = padded.at[:, :, first_col : first_col + width + SUPPORT].add(strip)
    partial_value = padded[:, :, :GRID_U]
    share = lax.psum_scatter(partial_value, "chan", scatter_dimension=2, tiled=True)
    carried = passed_along(share[:, TILE_V:, :], "tile", 1)
    result = share[:, :TILE_V, :] + jnp.pad(carried, ((0, 0), (0, TILE_V - SUPPORT), (0, 0)))
    return result


def solution(mesh):
    placed = (
        P(None, ("chan", "tile")),
        P(),
        P(("chan", "tile")),
        P(("chan", "tile"), None),
        P(("chan", "tile")),
        P(("chan", "tile")),
    )
    return jax.shard_map(
        body, mesh=mesh, in_specs=placed, out_specs=P(None, "tile", "chan"), check_vma=False
    )
```

profile of v0, /device:TPU:0, one launch (start us, length us, event | category | flops | bytes accessed | tf_op | source)
XLA Modules:
  0.0 109.5 jit_solution(6552209601166467978)
XLA Ops:
  6.5 0.7 compare_convert_fusion
  7.3 1.2 %reduce-window.6 = s32[4,2,128]{2,1,0:T(2,128)S(1)} reduce-window(s32[4,2,128]{2,1,0:T(2,128)S(1)} %compare_convert_fusion, s32[]{:T(128)} %constant.163.clone.1), window={size=1x1x128 pad=0_0x0_0x127_0}, to_apply=%region_0.0 | reduce-window | flops 130048 | bytes 8196 | tf_op jit(solution)/shard_map/reduce-window
  8.5 0.1 slice.262
  8.6 0.1 copy.111
  8.7 0.1 copy.112
  8.9 0.7 fusion.32
  9.6 0.7 compare_select_fusion
  10.3 2.1 %scatter_custom_fusion.1 = s32[512]{0:T(512)} fusion(s32[256]{0:T(256)S(1)} %bitcast.137, s32[256]{0:T(256)} %param.16, s32[]{:T(128)} %constant.163.clone.1), kind=kCustom, calls=%fused_computation.94 | custom fusion | bytes 2560 | tf_op jit(solution)/shard_map/scatter | solution.py:41
  12.4 6.3 %all-to-all-start.1 = ((s32[4,1,128]{2,1,0:T(1,128)}), s32[4,1,128]{2,1,0:T(1,128)S(1)}, u32[]{:S(2)}, u32[]{:S(2)}) async-start(s32[4,1,128]{2,1,0:T(1,128)} %bitcast.9), calls=%async_computation.1 | async-start | bytes 4096 | tf_op jit(solution)/shard_map/all_to_all | solution.py:50
  18.7 0.7 compare_and_fusion
  19.4 0.8 fusion.37
  20.2 0.9 gather_fusion
  21.0 0.1 select_convert_fusion
  21.1 0.2 subtract_convert_fusion
  21.3 1.3 %scatter_custom_fusion = bf16[512,128]{1,0:T(8,128)(2,1)S(1)} fusion(s32[256]{0:T(256)S(1)} %bitcast.138, bf16[256,64]{1,0:T(8,128)(2,1)S(1)} %get-tuple-element.90, bf16[]{:T(256)} %constant.248, bf16[256,64]{1,0:T(8,128)(2,1)S(1)} %get-tuple-element.89, bf16[]{:T(256)} %constant.161.clone.1), kind=kCustom, calls=%fused_computation.67 | custom fusion | flops 131072 | bytes 262148 | tf_op jit(solution)/shard_map/scatter | solution.py:40
  22.6 0.8 copy.113
  23.4 0.8 all-to-all-done.1
  24.2 4.3 %all-to-all-start = ((bf16[4,128,128]{1,2,0:T(8,128)(2,1)}), bf16[4,128,128]{1,2,0:T(8,128)(2,1)S(1)}, u32[]{:S(2)}, u32[]{:S(2)}) async-start(bf16[4,128,128]{1,2,0:T(8,128)(2,1)} %copy.113), calls=%async_computation | async-start | bytes 262144 | tf_op jit(solution)/shard_map/all_to_all | solution.py:43
  28.5 0.1 iota_add_fusion
  28.7 5.8 %all-to-all-done = bf16[4,128,128]{1,2,0:T(8,128)(2,1)S(1)} async-done(((bf16[4,128,128]{1,2,0:T(8,128)(2,1)}), bf16[4,128,128]{1,2,0:T(8,128)(2,1)S(1)}, u32[]{:S(2)}, u32[]{:S(2)}) %all-to-all-start) | async-done | bytes 131104 | tf_op jit(solution)/shard_map/all_to_all | solution.py:43
  34.4 0.1 copy.154
  34.6 3.4 %reshape.305 = bf16[512,2,8,8]{3,2,1,0:T(8,128)(2,1)} reshape(bf16[4,128,128]{2,1,0:T(8,128)(2,1)S(1)} %copy.154) | data formatting | bytes 262144 | tf_op jit(solution)/shard_map/reshape;reshape | solution.py:63
  37.9 2.3 %fusion.15 = bf16[512,2,8,24]{3,2,1,0:T(8,128)(2,1)S(1)} fusion(bf16[512,2,8,8]{3,2,1,0:T(8,128)(2,1)} %reshape.305, s32[512,8]{1,0:T(8,128)S(1)} %iota_add_fusion), kind=kOutput, calls=%fused_computation.18 | convolution fusion | flops 3440640 | bytes 540672 | tf_op jit(solution)/shard_map/rjy,rcij->rcyi/dot_general | solution.py:64
  40.2 2.0 %copy.116 = bf16[512,2,24,8]{0,3,2,1:T(8,128)(2,1)S(1)} copy(bf16[512,2,24,8]{2,3,1,0:T(8,128)(2,1)S(1)} %bitcast.125) | data formatting | bytes 786432 | tf_op jit(solution)/shard_map/convert_element_type | solution.py:65
  42.3 0.8 fusion.4
  43.1 2.2 %fusion.36 = (f32[2,24,1,1024]{3,2,1,0:T(1,128)S(1)}, f32[2,24,1,1024]{3,2,1,0:T(1,128)S(1)}, f32[2,24,1,1024]{3,2,1,0:T(1,128)}, f32[2,24,1,1024]{3,2,1,0:T(1,1...) fusion(f32[2,24,8,1024]{3,2,1,0:T(8,128)S(1)} %fusion.4), kind=kLoop, calls=%fused_computation.97 | loop fusion | bytes 3145728 | tf_op jit(solution)/shard_map/slice | solution.py:85
  45.4 2.3 %copy.150 = bf16[2,24,8,512]{3,1,0,2:T(8,128)(2,1)} copy(bf16[2,24,8,512]{1,2,0,3:T(8,128)(2,1)S(1)} %bitcast.126) | data formatting | bytes 786432 | tf_op jit(solution)/shard_map/dot_general | solution.py:76
  47.7 1.8 %fusion.7 = f32[2,24,8,1024]{3,1,0,2:T(8,128)S(1)} fusion(bf16[2,24,8,512]{3,1,0,2:T(8,128)(2,1)} %copy.150, s32[512]{0:T(512)S(1)} %get-tuple-element.92), kind=kOutput, calls=%fused_computation.13 | convolution fusion | flops 403177472 | bytes 1968128 | tf_op jit(solution)/shard_map/dot_general | solution.py:76
  49.5 0.2 slice_bitcast_fusion.23
  49.6 0.8 copy-done.10
  50.4 0.8 fusion.10
  51.2 1.2 %slice_bitcast_fusion.15 = (f32[2,24,1024]{2,1,0:T(8,128)}, f32[2,24,1024]{2,1,0:T(8,128)}, f32[2,24,1024]{2,1,0:T(8,128)}, f32[2,24,1024]{2,1,0:T(8,128)}, f32[...) fusion(f32[2,24,8,1024]{3,1,0,2:T(8,128)S(1)} %fusion.10), kind=kLoop, calls=%fused_computation.47 | loop fusion | bytes 3145728 | tf_op jit(solution)/shard_map/squeeze | solution.py:85
  52.4 0.8 fusion.13
  53.2 0.9 slice_bitcast_fusion.7
  54.1 0.3 copy-done.4
  54.5 0.1 copy-done.2
  54.7 0.5 pad_add_fusion
  55.3 0.5 fusion.24
  55.8 1.1 scatter-add.15
  56.9 1.8 %slice_add_fusion.1 = f32[2,24,1032]{2,1,0:T(8,128)S(1)} fusion(f32[2,24,4104]{2,1,0:T(8,128)S(1)} %scatter-add.15, f32[2,24,1024]{2,1,0:T(8,128)} %get-tuple-element.72, f32[2,24,1024]{2,1,0:T(8,128)S(1)} %copy-done.9, f32[2,24,1024]{2,1,0:T(8,128)} %get-tuple-element.67, f32[2,24,1024]{2,1,0:T(8,128)} %get-tuple-element.68, ...), kind=kLoop, calls=%fused_computation.30 | loop fusion | flops 396288 | bytes 1969152 | tf_op jit(solution)/shard_map/add | solution.py:86
  58.7 1.1 scatter-add.16
  59.8 0.5 fusion.25
  60.3 1.0 slice.299
  61.3 34.2 %reduce-scatter.2.cloned.1.call-done = f32[2,24,512]{2,1,0:T(8,128)} async-done(((f32[2,24,4096]{2,1,0:T(8,128)}), f32[2,24,512]{2,1,0:T(8,128)}) %reduce-scatter.2.cloned.1.call-update) | async-done | bytes 98320 | tf_op jit(solution)/shard_map/reduce_scatter | solution.py:88
  95.4 0.8 slice.301
  96.2 3.4 %collective-permute-start = (f32[2,8,512]{2,1,0:T(8,128)S(1)}, f32[2,8,512]{2,1,0:T(8,128)S(1)}, u32[]{:S(2)}, u32[]{:S(2)}) collective-permute-start(f32[2,8,512]{2,1,0:T(8,128)S(1)} %slice.301), channel_id=1, source_target_pairs={{0,1},{1,2},{2,3},{4,5},{5,6},{6,7},{8,9},{9,10},{10,11},{12,13},{... | collective-permute-start | bytes 98312 | tf_op jit(solution)/shard_map/ppermute | solution.py:17
  99.6 1.6 %collective-permute-done = f32[2,8,512]{2,1,0:T(8,128)S(1)} collective-permute-done((f32[2,8,512]{2,1,0:T(8,128)S(1)}, f32[2,8,512]{2,1,0:T(8,128)S(1)}, u32[]{:S(2)}, u32[]{:S(2)}) %collective-permute-start) | collective-permute-done | bytes 32800 | tf_op jit(solution)/shard_map/ppermute | solution.py:17
  101.2 1.5 %slice_add_fusion.2 = f32[2,16,512]{2,1,0:T(8,128)} fusion(f32[2,24,512]{2,1,0:T(8,128)} %reduce-scatter.2.cloned.1.call-done, f32[2,8,512]{2,1,0:T(8,128)S(1)} %collective-permute-done), kind=kLoop, calls=%fused_computation.66 | loop fusion | flops 16384 | bytes 163840 | tf_op jit(solution)/shard_map/add | solution.py:90
  (34 shorter events, 0.6 us)
Async XLA Ops:
  6.5 13.6 %copy-start = (bf16[2048,128]{1,0:T(8,128)(2,1)S(1)}, bf16[2048,128]{1,0:T(8,128)(2,1)}, u32[]{:S(2)}) copy-start(bf16[2048,128]{1,0:T(8,128)(2,1)} %param.15) | copy-start | bytes 1572868
  12.4 11.8 %all-to-all-start.1 = ((s32[4,1,128]{2,1,0:T(1,128)}), s32[4,1,128]{2,1,0:T(1,128)S(1)}, u32[]{:S(2)}, u32[]{:S(2)}) async-start(s32[4,1,128]{2,1,0:T(1,128)} %bitcast.9), calls=%async_computation.1 | async-start | bytes 4096 | tf_op jit(solution)/shard_map/all_to_all | solution.py:50
  24.2 10.2 %all-to-all-start = ((bf16[4,128,128]{1,2,0:T(8,128)(2,1)}), bf16[4,128,128]{1,2,0:T(8,128)(2,1)S(1)}, u32[]{:S(2)}, u32[]{:S(2)}) async-start(bf16[4,128,128]{1,2,0:T(8,128)(2,1)} %copy.113), calls=%async_computation | async-start | bytes 262144 | tf_op jit(solution)/shard_map/all_to_all | solution.py:43
  28.5 67.0 %reduce-scatter.2.cloned.1.call-start = ((), (), s32[]{:S(2)}) async-start(), calls=%async_computation.3 | async-start | bytes 884736 | tf_op jit(solution)/shard_map/reduce_scatter | solution.py:88
  49.4 1.0 copy-start.10
  53.1 1.0 copy-start.3
  53.1 1.2 %copy-start.4 = (f32[2,24,1,1024]{3,2,1,0:T(1,128)S(1)}, f32[2,24,1,1024]{3,2,1,0:T(1,128)}, u32[]{:S(2)}) copy-start(f32[2,24,1,1024]{3,2,1,0:T(1,128)} %get-tuple-element.86) | copy-start | bytes 589828
  53.1 1.3 %copy-start.1 = (f32[2,24,1,1024]{3,2,1,0:T(1,128)S(1)}, f32[2,24,1,1024]{3,2,1,0:T(1,128)}, u32[]{:S(2)}) copy-start(f32[2,24,1,1024]{3,2,1,0:T(1,128)} %get-tuple-element.83) | copy-start | bytes 589828
  53.2 1.4 %copy-start.2 = (f32[2,24,1,1024]{3,2,1,0:T(1,128)S(1)}, f32[2,24,1,1024]{3,2,1,0:T(1,128)}, u32[]{:S(2)}) copy-start(f32[2,24,1,1024]{3,2,1,0:T(1,128)} %get-tuple-element.84) | copy-start | bytes 589828
  55.2 1.7 %copy-start.8 = (f32[2,24,1024]{2,1,0:T(8,128)S(1)}, f32[2,24,1024]{2,1,0:T(8,128)}, u32[]{:S(2)}) copy-start(f32[2,24,1024]{2,1,0:T(8,128)} %get-tuple-element.65) | copy-start | bytes 589828
  55.2 1.7 %copy-start.9 = (f32[2,24,1024]{2,1,0:T(8,128)S(1)}, f32[2,24,1024]{2,1,0:T(8,128)}, u32[]{:S(2)}) copy-start(f32[2,24,1024]{2,1,0:T(8,128)} %get-tuple-element.66) | copy-start | bytes 589828
  55.3 4.5 %copy-start.5 = (f32[2,24,1024]{2,1,0:T(8,128)S(1)}, f32[2,24,1024]{2,1,0:T(8,128)}, u32[]{:S(2)}) copy-start(f32[2,24,1024]{2,1,0:T(8,128)} %get-tuple-element.62) | copy-start | bytes 589828
  55.3 4.5 %copy-start.6 = (f32[2,24,1024]{2,1,0:T(8,128)S(1)}, f32[2,24,1024]{2,1,0:T(8,128)}, u32[]{:S(2)}) copy-start(f32[2,24,1024]{2,1,0:T(8,128)} %get-tuple-element.63) | copy-start | bytes 589828
  55.3 4.5 %copy-start.7 = (f32[2,24,1024]{2,1,0:T(8,128)S(1)}, f32[2,24,1024]{2,1,0:T(8,128)}, u32[]{:S(2)}) copy-start(f32[2,24,1024]{2,1,0:T(8,128)} %get-tuple-element.64) | copy-start | bytes 589828
  96.2 5.0 %collective-permute-start = (f32[2,8,512]{2,1,0:T(8,128)S(1)}, f32[2,8,512]{2,1,0:T(8,128)S(1)}, u32[]{:S(2)}, u32[]{:S(2)}) collective-permute-start(f32[2,8,512]{2,1,0:T(8,128)S(1)} %slice.301), channel_id=1, source_target_pairs={{0,1},{1,2},{2,3},{4,5},{5,6},{6,7},{8,9},{9,10},{10,11},{12,13},{... | collective-permute-start | bytes 98312 | tf_op jit(solution)/shard_map/ppermute | solution.py:17
Sparse Core Ops, SparseCore 0:
  61.4 34.0 reduce-scatter.1
where the time goes:
time: 110 us; the launch traced here: 109 us
  waiting for transfers between devices  42.3 us (38%)
  local copies, waits for them, and re-layouts  22.6 us (21%)
  starting transfers between devices  14 us (13%)
  between operations  13.7 us (12%)
  other arithmetic  10.6 us (10%)
  matrix products  6.32 us (6%)
    reduce_scatter x1, waiting for transfers between devices, body(): lax.psum_scatter(partial_value, 'chan', scatter_dimension=2, tiled=True)  34.2 us
    all_to_all x1, starting transfers between devices, body(): lax.all_to_all(send_cells.reshape(tiles, CAPACITY), 'tile', split_axis=0,...  6.32 us
    all_to_all x1, waiting for transfers between devices, body(): lax.all_to_all(send_values.reshape(tiles, CAPACITY, 2 * area), 'tile', sp...  5.76 us
    all_to_all x1, starting transfers between devices, body(): lax.all_to_all(send_values.reshape(tiles, CAPACITY, 2 * area), 'tile', sp...  4.33 us
    dot_general x4, matrix products, body(): lax.dot_general(spread[first_row:first_row + block], onehot, (((0,), (0,)...  4.02 us
    another operation x2, local copies, waits for them, and re-layouts, body(): values = weighted_all.reshape(slots, 2, SUPPORT, SUPPORT)  3.51 us
    ppermute x1, starting transfers between devices, passed_along(): return lax.ppermute(shard, axis, pairs)  3.38 us
    squeeze x6, local copies, waits for them, and re-layouts, body(): section[:, :, tap, :]  2.4 us
  transfers between devices with their start and end apart: 4, of which 4 were waited for; matrix products, arithmetic and copies ran while one was open for 4% of the time, Pallas kernels for 0%

commit v1 on v0

v1 whole, which is shorter than its diff:
```python
import functools

import jax
import jax.numpy as jnp
from jax import lax
from jax.experimental import pallas as pl
from jax.experimental.pallas import tpu as pltpu
from jax.sharding import PartitionSpec as P

GRID_U = 4096
SUPPORT = 8
OVERSAMPLE = 8
TILE_V = 16
AREA = SUPPORT * SUPPORT
LANES = 128
BLOCK = 2 * LANES
CHUNK = 768
PIECE = 256


def pack_kernel(vis_ref, cell_ref, tile_ref, plane_ref, offset_ref, out_ref):
    rows = vis_ref.shape[1]
    address = (tile_ref[...] * (TILE_V * GRID_U) + cell_ref[...]).astype(jnp.float32)
    kind = (plane_ref[...] * (OVERSAMPLE * OVERSAMPLE) + offset_ref[...]).astype(jnp.float32)
    parts = []
    for first in range(0, rows, BLOCK):
        for q in range(2):
            for half in range(2):
                start = first + half * LANES
                parts.append(vis_ref[q : q + 1, start : start + LANES])
        at = first // LANES
        parts.append(address[at : at + 2])
        parts.append(kind[at : at + 2])
    packed = jnp.concatenate(parts, axis=0)

    @pl.loop(0, out_ref.shape[0])
    def _(d):
        out_ref[d] = packed


def pack(devices, visibility, cell, tile, plane, offset):
    rows = visibility.shape[1]
    flat = [a.reshape(rows // LANES, LANES) for a in (cell, tile, plane, offset)]
    return pl.pallas_call(
        pack_kernel,
        out_shape=jax.ShapeDtypeStruct((devices, rows // BLOCK * 8, LANES), jnp.float32),
        in_specs=[pl.BlockSpec(memory_space=pltpu.VMEM)] * 5,
        out_specs=pl.BlockSpec(memory_space=pltpu.VMEM),
        compiler_params=pltpu.CompilerParams(vmem_limit_bytes=32 * 1024 * 1024),
    )(visibility, *flat)


def along_lanes(values, index):
    return jnp.take_along_axis(values, index, axis=1, mode="promise_in_bounds")


def along_sublanes(values, index):
    return jnp.take_along_axis(values, index, axis=0, mode="promise_in_bounds")


def iota(shape, axis):
    return lax.broadcasted_iota(jnp.int32, shape, axis)


def dot(a, b, dims):
    return lax.dot_general(a, b, (dims, ((), ())), preferred_element_type=jnp.float32)


def grid_kernel(span, rows_ref, table_ref, out_ref, total_ref):
    width = out_ref.shape[2]
    blocks = rows_ref.shape[0] // 8
    groups = 2 * span
    first_u = lax.axis_index("chan") * width
    first_v = lax.axis_index("tile") * TILE_V
    total_ref[...] = jnp.zeros_like(total_ref)
    upper = (iota((LANES, LANES), 0) <= iota((LANES, LANES), 1)).astype(jnp.float32).astype(jnp.bfloat16)
    ones = jnp.ones((LANES, LANES), jnp.bfloat16)
    before = (iota((groups, groups), 1) < iota((groups, groups), 0)).astype(jnp.float32).astype(jnp.bfloat16)

    def section(first_block):
        def column(q):
            return jnp.concatenate(
                [rows_ref[pl.ds(first_block * 8 + q * 2 + half, span, stride=8), :] for half in range(2)],
                axis=0,
            )

        real, imag, address, kind = [column(q) for q in range(4)]
        whole = address.astype(jnp.int32)
        v_rel = (whole >> 12) - first_v
        u_rel = (whole & (GRID_U - 1)) - first_u
        touches = (v_rel > -SUPPORT) & (v_rel < TILE_V) & (u_rel > -SUPPORT) & (u_rel < width)
        marks = jnp.where(touches, 1.0, 0.0).astype(jnp.bfloat16)
        upto = dot(marks, upper, ((1,), (0,))).astype(jnp.int32)
        count = dot(marks, ones, ((1,), (0,)))
        base = dot(before, count.astype(jnp.bfloat16), ((1,), (0,))).astype(jnp.int32)
        count = count.astype(jnp.int32)
        picked = jnp.max(base + count)
        lane = iota((groups, LANES), 1)
        source = jnp.zeros((groups, LANES), jnp.int32)
        step = LANES // 2
        while step:
            probe = along_lanes(upto, source + (step - 1))
            source = jnp.where(probe <= lane, source + step, source)
            step //= 2

        def chunk(number, carry):
            lists = [[], [], [], []]
            for piece in range(CHUNK // LANES):
                place = lane + (number * CHUNK + piece * LANES) - base
                here = (place >= 0) & (place < count)
                at = along_lanes(source, place & (LANES - 1))
                for q, values in enumerate((real, imag, address, kind)):
                    got = jnp.where(here, along_lanes(values, at), 0.0)
                    lists[q].append(jnp.sum(got, axis=0, keepdims=True))
            for piece in range(CHUNK // PIECE):
                each = PIECE // LANES
                vr, vi, address_n, kind_n = [
                    jnp.concatenate(l[piece * each : (piece + 1) * each], axis=1) for l in lists
                ]
                whole_n = address_n.astype(jnp.int32)
                v_n = (whole_n >> 12) - first_v
                u_n = (whole_n & (GRID_U - 1)) - first_u
                kind_i = kind_n.astype(jnp.int32)
                low = kind_i & 255
                high = kind_i >> 8
                onehot = jnp.where(iota((256, PIECE), 0) == low, 1.0, 0.0).astype(jnp.bfloat16)
                kern = jnp.zeros((2 * AREA, PIECE), jnp.float32)
                for t in range(table_ref.shape[0] // (2 * AREA)):
                    part = dot(table_ref[t * 2 * AREA : (t + 1) * 2 * AREA, :], onehot, ((1,), (0,)))
                    kern = kern + jnp.where(high == t, part, 0.0)
                real_kern = kern[:AREA]
                imag_kern = kern[AREA:]
                weighted = (vr * real_kern - vi * imag_kern, vr * imag_kern + vi * real_kern)
                sub = iota((SUPPORT, PIECE), 0)
                turn = (sub - v_n) & (SUPPORT - 1)
                inside = [(sub + 8 * y >= v_n) & (sub + 8 * y < v_n + SUPPORT) for y in range(2)]
                spread = []
                for i in range(SUPPORT):
                    in_u = (u_n + i >= 0) & (u_n + i < width)
                    for c in range(2):
                        turned = along_sublanes(weighted[c][i * 8 : (i + 1) * 8], turn)
                        for y in range(2):
                            spread.append(jnp.where(inside[y] & in_u, turned, 0.0))
                spread = jnp.concatenate(spread, axis=0).astype(jnp.bfloat16)
                column_n = jnp.where(u_n < 0, u_n + width, u_n)
                place_u = jnp.where(iota((width, PIECE), 0) == column_n, 1.0, 0.0).astype(jnp.bfloat16)
                total_ref[...] += dot(spread, place_u, ((1,), (1,)))
            return carry

        lax.fori_loop(0, (picked + CHUNK - 1) // CHUNK, chunk, 0)

    if blocks == span:
        section(0)
    else:
        pl.loop(0, blocks // span)(lambda s: section(s * span))
    both = 2 * TILE_V
    result = total_ref[0:both, :]
    for i in range(1, SUPPORT):
        result = result + pltpu.roll(total_ref[i * both : (i + 1) * both, :], i, axis=1)
    out_ref[0] = result[:TILE_V]
    out_ref[1] = result[TILE_V:]


def body(visibility, kernel_table, cell_index, tile_index, plane_index, offset_index):
    chans, tiles = lax.axis_size("chan"), lax.axis_size("tile")
    devices = chans * tiles
    packed = pack(devices, visibility, cell_index, tile_index[:, 0], plane_index, offset_index)
    arrived = lax.all_to_all(packed, ("chan", "tile"), split_axis=0, concat_axis=0)
    kernels = kernel_table.shape[0]
    table = kernel_table.reshape(kernels // 256, 256, 2 * AREA).transpose(0, 2, 1).reshape(-1, 256)
    rows = arrived.reshape(-1, LANES)
    blocks = rows.shape[0] // 8
    span = 32 if blocks % 32 == 0 else blocks
    width = GRID_U // chans
    return pl.pallas_call(
        functools.partial(grid_kernel, span),
        out_shape=jax.ShapeDtypeStruct((2, TILE_V, width), jnp.float32),
        in_specs=[pl.BlockSpec(memory_space=pltpu.VMEM)] * 2,
        out_specs=pl.BlockSpec(memory_space=pltpu.VMEM),
        scratch_shapes=[pltpu.VMEM((2 * TILE_V * SUPPORT, width), jnp.float32)],
        compiler_params=pltpu.CompilerParams(vmem_limit_bytes=32 * 1024 * 1024),
    )(rows, table)


def solution(mesh):
    placed = (
        P(None, ("chan", "tile")),
        P(),
        P(("chan", "tile")),
        P(("chan", "tile"), None),
        P(("chan", "tile")),
        P(("chan", "tile")),
    )
    return jax.shard_map(
        body, mesh=mesh, in_specs=placed, out_specs=P(None, "tile", "chan"), check_vma=False
    )
```

time: 110 us -> 20.5 us (0.19)
  waiting for transfers between devices: 42.3 us -> 7.15 us
  local copies, waits for them, and re-layouts: 22.6 us -> 1.98 us
  between operations: 13.7 us -> 0.03 us
  other arithmetic: 10.6 us -> 0 us
  starting transfers between devices: 14 us -> 7.3 us
  matrix products: 6.32 us -> 0 us
  Pallas kernels: 0 us -> 3.84 us
    reduce_scatter x1 -> x0, waiting for transfers between devices: 34.2 us -> none  [body(): lax.psum_scatter(partial_value, 'chan', scatter_dimension=2, tiled=True)]
    dot_general x5 -> x0, matrix products: 6.32 us -> none  [the longest x4 4.02 us: body(): lax.dot_general(spread[first_row:first_row + block], onehot, (((0,), (0,)...]
    slice x4 -> x0, local copies, waits for them, and re-layouts: 4.7 us -> none  [the longest x1 2.22 us: body(): section[:, :, tap, :]]
    add x5 -> x0, other arithmetic: 4.35 us -> none  [the longest x2 2.27 us: body(): padded = padded.at[:, :, first_col:first_col + width + SUPPORT].add(strip)]
    pallas_call x0 -> x2, Pallas kernels: none -> 3.84 us  [the longest x1 3.01 us: body(): pl.pallas_call(functools.partial(grid_kernel, span), out_shape=jax.ShapeD...]
    another operation x6 -> x0, local copies, waits for them, and re-layouts: 3.79 us -> none  [the longest x2 3.51 us: body(): values = weighted_all.reshape(slots, 2, SUPPORT, SUPPORT)]
    ppermute x1 -> x0, starting transfers between devices: 3.38 us -> none  [passed_along(): return lax.ppermute(shard, axis, pairs)]
    all_to_all x2 -> x1, starting transfers between devices: 10.6 us -> 7.3 us  [body(): lax.all_to_all(packed, ('chan', 'tile'), split_axis=0, concat_axis=0)]
  transfers between devices with their start and end apart: 4 -> 1, of which waited for: 4 -> 1; matrix products, arithmetic and copies ran while one was open for 4% -> 6% of each run, Pallas kernels for 0% -> 0%
where the time goes in v1:
time: 20.5 us; the launch traced here: 20.3 us
  starting transfers between devices  7.3 us (36%)
  waiting for transfers between devices  7.15 us (35%)
  Pallas kernels  3.84 us (19%)
  local copies, waits for them, and re-layouts  1.98 us (10%)
    all_to_all x1, starting transfers between devices, body(): lax.all_to_all(packed, ('chan', 'tile'), split_axis=0, concat_axis=0)  7.3 us
    all_to_all x1, waiting for transfers between devices, body(): lax.all_to_all(packed, ('chan', 'tile'), split_axis=0, concat_axis=0)  7.15 us
    pallas_call x1, Pallas kernels, body(): pl.pallas_call(functools.partial(grid_kernel, span), out_shape=jax.ShapeD...  3.01 us
    reshape x1, local copies, waits for them, and re-layouts, body(): kernel_table.reshape(kernels // 256, 256, 2 * AREA).transpose(0, 2, 1)  1.25 us
    pallas_call x1, Pallas kernels, pack(): pl.pallas_call(pack_kernel, out_shape=jax.ShapeDtypeStruct((devices, rows...  0.82 us
    unnamed x10, local copies, waits for them, and re-layouts  0.73 us
  transfers between devices with their start and end apart: 1, of which 1 were waited for; matrix products, arithmetic and copies ran while one was open for 6% of the time, Pallas kernels for 0%

profile of v1, /device:TPU:0, one launch (start us, length us, event | category | flops | bytes accessed | tf_op | source)
XLA Modules:
  0.0 20.3 jit_solution(15935646665390285869)
XLA Ops:
  0.0 0.0 copy-start.4
  0.0 0.0 copy-start.2
  0.0 0.0 copy-start.3
  0.0 0.0 copy-start
  0.0 0.0 copy-start.1
  0.0 0.7 %copy-done.4 = s32[256]{0:T(256)S(1)} copy-done((s32[256]{0:T(256)S(1)}, s32[256]{0:T(256)}, u32[]{:S(2)}) %copy-start.4) | copy-done | bytes 1048
  0.7 0.0 copy-done.2
  0.7 0.0 copy-done.3
  0.7 0.0 copy-done
  0.7 0.0 copy-done.1
  0.7 0.8 %shard_map.64 = f32[32,8,128]{2,1,0:T(8,128)} custom-call(f32[2,256]{1,0:T(2,128)S(1)} %copy-done, s32[2,128]{1,0:T(2,128)S(1)} %bitcast.11, s32[2,128]{1,0:T(2,128)S(1)} %bitcast.12, s32[2,128]{1,0:T(2,128)S(1)} %bitcast.13, s32[2,128]{1,0:T(2,128)S(1)} %bitcast.14), custom_call_target="tpu_custom_call" | custom-call | tf_op jit(solution)/shard_map/pallas_call | solution.py:44
  1.6 7.3 %all-to-all-start = ((f32[32,8,128]{2,1,0:T(8,128)}), f32[32,8,128]{2,1,0:T(8,128)S(1)}, u32[]{:S(2)}, u32[]{:S(2)}) async-start(f32[32,8,128]{2,1,0:T(8,128)} %shard_map.64), calls=%async_computation | async-start | bytes 262144 | tf_op jit(solution)/shard_map/all_to_all | solution.py:168
  8.9 1.2 %copy.7 = bf16[8,256,128]{1,2,0:T(8,128)(2,1)S(1)} copy(bf16[8,256,128]{2,1,0:T(8,128)(2,1)} %bitcast.15) | data formatting | bytes 1048576 | tf_op jit(solution)/shard_map/reshape | solution.py:170
  10.1 7.2 %all-to-all-done = f32[32,8,128]{2,1,0:T(8,128)S(1)} async-done(((f32[32,8,128]{2,1,0:T(8,128)}), f32[32,8,128]{2,1,0:T(8,128)S(1)}, u32[]{:S(2)}, u32[]{:S(2)}) %all-to-all-start) | async-done | bytes 131104 | tf_op jit(solution)/shard_map/all_to_all | solution.py:168
  17.3 3.0 %shard_map.65 = f32[2,16,512]{2,1,0:T(8,128)} custom-call(f32[256,128]{1,0:T(8,128)S(1)} %bitcast.10, bf16[1024,256]{1,0:T(8,128)(2,1)S(1)} %bitcast.9), custom_call_target="tpu_custom_call" | custom-call | tf_op jit(solution)/shard_map/pallas_call | solution.py:175
Async XLA Ops:
  0.0 0.7 %copy-start.4 = (s32[256]{0:T(256)S(1)}, s32[256]{0:T(256)}, u32[]{:S(2)}) copy-start(s32[256]{0:T(256)} %param.11) | copy-start | bytes 3076
  0.0 0.7 %copy-start.2 = (s32[256,1]{0,1:T(1,128)S(1)}, s32[256,1]{0,1:T(1,128)}, u32[]{:S(2)}) copy-start(s32[256,1]{0,1:T(1,128)} %param.9) | copy-start | bytes 3076
  0.0 0.7 %copy-start.3 = (s32[256]{0:T(256)S(1)}, s32[256]{0:T(256)}, u32[]{:S(2)}) copy-start(s32[256]{0:T(256)} %param.10) | copy-start | bytes 3076
  0.0 0.7 %copy-start = (f32[2,256]{1,0:T(2,128)S(1)}, f32[2,256]{1,0:T(2,128)}, u32[]{:S(2)}) copy-start(f32[2,256]{1,0:T(2,128)} %vis_ref.1) | copy-start | bytes 6148
  0.0 0.7 %copy-start.1 = (s32[256]{0:T(256)S(1)}, s32[256]{0:T(256)}, u32[]{:S(2)}) copy-start(s32[256]{0:T(256)} %param.8) | copy-start | bytes 3076
  1.6 15.7 %all-to-all-start = ((f32[32,8,128]{2,1,0:T(8,128)}), f32[32,8,128]{2,1,0:T(8,128)S(1)}, u32[]{:S(2)}, u32[]{:S(2)}) async-start(f32[32,8,128]{2,1,0:T(8,128)} %shard_map.64), calls=%async_computation | async-start | bytes 262144 | tf_op jit(solution)/shard_map/all_to_all | solution.py:168

commit v2 on v1

v2 whole, which is shorter than its diff:
```python
import functools

import jax
import jax.numpy as jnp
from jax import lax
from jax.experimental import pallas as pl
from jax.experimental.pallas import tpu as pltpu
from jax.sharding import PartitionSpec as P

GRID_U = 4096
SUPPORT = 8
OVERSAMPLE = 8
TILE_V = 16
AREA = SUPPORT * SUPPORT
LANES = 128
BLOCK = 2 * LANES
PLAIN = 4
PIECE = 256


def pack_kernel(vis_ref, cell_ref, tile_ref, plane_ref, offset_ref, out_ref):
    rows = vis_ref.shape[1]
    address = (tile_ref[...] * (TILE_V * GRID_U) + cell_ref[...]).astype(jnp.float32)
    kind = (plane_ref[...] * (OVERSAMPLE * OVERSAMPLE) + offset_ref[...]).astype(jnp.float32)
    parts = []
    for first in range(0, rows, BLOCK):
        for q in range(2):
            for half in range(2):
                start = first + half * LANES
                parts.append(vis_ref[q : q + 1, start : start + LANES])
        at = first // LANES
        parts.append(address[at : at + 2])
        parts.append(kind[at : at + 2])
    packed = jnp.concatenate(parts, axis=0)

    for d in range(out_ref.shape[0]):
        out_ref[d] = packed


def pack(devices, visibility, cell, tile, plane, offset):
    rows = visibility.shape[1]
    flat = [a.reshape(rows // LANES, LANES) for a in (cell, tile, plane, offset)]
    return pl.pallas_call(
        pack_kernel,
        out_shape=jax.ShapeDtypeStruct((devices, rows // BLOCK * 8, LANES), jnp.float32),
        in_specs=[pl.BlockSpec(memory_space=pltpu.VMEM)] * 5,
        out_specs=pl.BlockSpec(memory_space=pltpu.VMEM),
        compiler_params=pltpu.CompilerParams(vmem_limit_bytes=4 * 1024 * 1024),
    )(visibility, *flat)


def along_lanes(values, index):
    return jnp.take_along_axis(values, index, axis=1, mode="promise_in_bounds")


def along_sublanes(values, index):
    return jnp.take_along_axis(values, index, axis=0, mode="promise_in_bounds")


def iota(shape, axis):
    return lax.broadcasted_iota(jnp.int32, shape, axis)


def dot(a, b, dims):
    return lax.dot_general(a, b, (dims, ((), ())), preferred_element_type=jnp.float32)


def ranks_down(marks):
    sub = iota((8, LANES), 0)
    above = jnp.zeros((8, LANES), jnp.int32)
    ranks = []
    for tile in marks:
        run = tile
        for by in (1, 2, 4):
            run = run + jnp.where(sub >= by, pltpu.roll(run, by, axis=0), 0)
        ranks.append(above + run - tile)
        above = above + jnp.broadcast_to(run[7:8], run.shape)
    return ranks, above


def grid_kernel(span, rows_ref, table_ref, out_ref, total_ref):
    width = out_ref.shape[2]
    blocks = rows_ref.shape[0] // 8
    first_u = lax.axis_index("chan") * width
    first_v = lax.axis_index("tile") * TILE_V
    sub = iota((8, LANES), 0)

    def section(first_block, fresh):
        def column(q, first):
            return rows_ref[pl.ds(first_block * 8 + first * 8 + q, 8, stride=8), :]

        real, imag, code, marks = [], [], [], []
        for half in range(2):
            for first in range(0, span, 8):
                real.append(column(half, first))
                imag.append(column(2 + half, first))
                address = column(4 + half, first).astype(jnp.int32)
                kind = column(6 + half, first).astype(jnp.int32)
                v_rel = (address >> 12) - first_v
                u_rel = (address & (GRID_U - 1)) - first_u
                touches = (v_rel > -SUPPORT) & (v_rel < TILE_V) & (u_rel > -SUPPORT) & (u_rel < width)
                marks.append(jnp.where(touches, 1, 0))
                code.append(kind + ((u_rel + SUPPORT) << 11) + ((v_rel + SUPPORT) << 24))
        ranks, total = ranks_down(marks)
        ranks = [jnp.where(m > 0, r, -1) for m, r in zip(marks, ranks)]
        lines = [[jnp.broadcast_to(r[j : j + 1], r.shape) for j in range(8)] for r in ranks]

        def pick(wanted):
            got = [jnp.zeros((8, LANES), x[0].dtype) for x in (real, imag, code)]
            for k, line in enumerate(lines):
                source = jnp.full((8, LANES), -1, jnp.int32)
                for j in range(8):
                    source = jnp.where(line[j] == wanted, j, source)
                for q, x in enumerate((real, imag, code)):
                    got[q] = jnp.where(source >= 0, along_sublanes(x[k], source & 7), got[q])
            return got

        def split(tiles, count):
            return [[tiles[q][r : r + 1] for r in range(count)] for q in range(3)]

        def add_up(lists, fresh):
            spreads, places = [], []
            for first in range(0, len(lists[0]), PIECE // LANES):
                vr, vi, code_n = [jnp.concatenate(l[first : first + PIECE // LANES], axis=1) for l in lists]
                kind_n = code_n & 2047
                u_n = ((code_n >> 11) & 8191) - SUPPORT
                v_n = (code_n >> 24) - SUPPORT
                low = kind_n & 255
                high = kind_n >> 8
                onehot = jnp.where(iota((256, PIECE), 0) == low, 1.0, 0.0).astype(jnp.bfloat16)
                kern = jnp.zeros((2 * AREA, PIECE), jnp.float32)
                for t in range(table_ref.shape[0] // (2 * AREA)):
                    part = dot(table_ref[t * 2 * AREA : (t + 1) * 2 * AREA, :], onehot, ((1,), (0,)))
                    kern = jnp.where(high == t, part, kern)
                real_kern = kern[:AREA]
                imag_kern = kern[AREA:]
                weighted = (vr * real_kern - vi * imag_kern, vr * imag_kern + vi * real_kern)
                sub_n = iota((SUPPORT, PIECE), 0)
                turn = (sub_n - v_n) & (SUPPORT - 1)
                inside = [(sub_n + 8 * y >= v_n) & (sub_n + 8 * y < v_n + SUPPORT) for y in range(2)]
                spread = []
                for i in range(SUPPORT):
                    in_u = (u_n + i >= 0) & (u_n + i < width)
                    for c in range(2):
                        turned = along_sublanes(weighted[c][i * 8 : (i + 1) * 8], turn)
                        for y in range(2):
                            spread.append(jnp.where(inside[y] & in_u, turned, 0.0))
                spreads.append(jnp.concatenate(spread, axis=0).astype(jnp.bfloat16))
                column_n = jnp.where(u_n < 0, u_n + width, u_n)
                places.append(jnp.where(iota((width, PIECE), 0) == column_n, 1.0, 0.0).astype(jnp.bfloat16))
            sums = dot(jnp.concatenate(spreads, axis=1), jnp.concatenate(places, axis=1), ((1,), (1,)))
            if fresh:
                total_ref[...] = sums
            else:
                total_ref[...] += sums

        beyond = jnp.maximum(total - PLAIN, 0)
        lane = iota((LANES, LANES), 0)
        other = iota((LANES, LANES), 1)
        left = jnp.where(((lane & 15) == (other & 15)) & (lane < other), 1.0, 0.0).astype(jnp.bfloat16)
        skip = dot(beyond.astype(jnp.float32).astype(jnp.bfloat16), left, ((1,), (0,))).astype(jnp.int32)
        lists = split(pick(sub), PLAIN)
        group = iota((8, LANES), 1) >> 4
        for first in (0, 8):
            wanted = sub + first - skip
            shared = pick(jnp.where(wanted >= 0, wanted + PLAIN, -2))
            for q, x in enumerate(shared):
                for by in (16, 32, 64):
                    x = x + pltpu.roll(x, by, axis=1)
                x = jnp.where(group == sub, x, jnp.zeros_like(x))
                for by in (1, 2, 4):
                    x = x + pltpu.roll(x, by, axis=0)
                lists[q].append(x[0:1])
        add_up(lists, fresh)
        done = PLAIN + jnp.maximum(16 - skip, 0)
        most = jnp.max(total - done)

        @pl.loop(0, (most + 7) // 8)
        def _(number):
            add_up(split(pick(sub + done + number * 8), 8), False)

    section(0, True)
    if blocks > span:
        pl.loop(1, blocks // span)(lambda s: section(s * span, False))
    both = 2 * TILE_V
    result = total_ref[0:both, :]
    for i in range(1, SUPPORT):
        result = result + pltpu.roll(total_ref[i * both : (i + 1) * both, :], i, axis=1)
    out_ref[0] = result[:TILE_V]
    out_ref[1] = result[TILE_V:]


def table_of(kernel_table):
    kernels = kernel_table.shape[0]
    return kernel_table.reshape(kernels // 256, 256, 2 * AREA).transpose(0, 2, 1).reshape(-1, 256)


def grid(arrived, table, chans):
    rows = arrived.reshape(-1, LANES)
    blocks = rows.shape[0] // 8
    span = 32 if blocks % 32 == 0 else blocks
    width = GRID_U // chans
    return pl.pallas_call(
        functools.partial(grid_kernel, span),
        out_shape=jax.ShapeDtypeStruct((2, TILE_V, width), jnp.float32),
        in_specs=[pl.BlockSpec(memory_space=pltpu.VMEM)] * 2,
        out_specs=pl.BlockSpec(memory_space=pltpu.VMEM),
        scratch_shapes=[pltpu.VMEM((2 * TILE_V * SUPPORT, width), jnp.float32)],
        compiler_params=pltpu.CompilerParams(vmem_limit_bytes=32 * 1024 * 1024),
    )(rows, table)


def body(visibility, kernel_table, cell_index, tile_index, plane_index, offset_index):
    chans, tiles = lax.axis_size("chan"), lax.axis_size("tile")
    packed = pack(chans * tiles, visibility, cell_index, tile_index[:, 0], plane_index, offset_index)
    first = (chans - 1) // 2 * 2 * tiles + tiles - 1
    order = [first] + [c * tiles + t for t in range(tiles) for c in range(chans) if c * tiles + t != first]
    arrived = lax.all_to_all(
        packed, ("chan", "tile"), split_axis=0, concat_axis=0, axis_index_groups=[order]
    )
    return grid(arrived, table_of(kernel_table), chans)


def solution(mesh):
    placed = (
        P(None, ("chan", "tile")),
        P(),
        P(("chan", "tile")),
        P(("chan", "tile"), None),
        P(("chan", "tile")),
        P(("chan", "tile")),
    )
    return jax.shard_map(
        body, mesh=mesh, in_specs=placed, out_specs=P(None, "tile", "chan"), check_vma=False
    )
```

time: 20.5 us -> 18.6 us (0.907)
  Pallas kernels: 3.84 us -> 2.68 us
  waiting for transfers between devices: 7.15 us -> 6.23 us
    pallas_call x1, Pallas kernels: 3.01 us -> 2.02 us  [grid(): pl.pallas_call(functools.partial(grid_kernel, span), out_shape=jax.ShapeD...]
    all_to_all x1, waiting for transfers between devices: 7.15 us -> 6.23 us  [body(): lax.all_to_all(packed, ('chan', 'tile'), split_axis=0, concat_axis=0, axi...]
  transfers between devices with their start and end apart: 1 -> 1, of which waited for: 1 -> 1; matrix products, arithmetic and copies ran while one was open for 6% -> 7% of each run, Pallas kernels for 0% -> 0%
where the time goes in v2:
time: 18.6 us; the launch traced here: 18.2 us
  starting transfers between devices  7.3 us (39%)
  waiting for transfers between devices  6.23 us (33%)
  Pallas kernels  2.68 us (14%)
  local copies, waits for them, and re-layouts  1.98 us (11%)
    all_to_all x1, starting transfers between devices, body(): lax.all_to_all(packed, ('chan', 'tile'), split_axis=0, concat_axis=0, axi...  7.3 us
    all_to_all x1, waiting for transfers between devices, body(): lax.all_to_all(packed, ('chan', 'tile'), split_axis=0, concat_axis=0, axi...  6.23 us
    pallas_call x1, Pallas kernels, grid(): pl.pallas_call(functools.partial(grid_kernel, span), out_shape=jax.ShapeD...  2.02 us
    reshape x1, local copies, waits for them, and re-layouts, table_of(): kernel_table.reshape(kernels // 256, 256, 2 * AREA).transpose(0, 2, 1)  1.25 us
    unnamed x10, local copies, waits for them, and re-layouts  0.73 us
    pallas_call x1, Pallas kernels, pack(): pl.pallas_call(pack_kernel, out_shape=jax.ShapeDtypeStruct((devices, rows...  0.66 us
  transfers between devices with their start and end apart: 1, of which 1 were waited for; matrix products, arithmetic and copies ran while one was open for 7% of the time, Pallas kernels for 0%

profile of v2, /device:TPU:0, one launch (start us, length us, event | category | flops | bytes accessed | tf_op | source)
XLA Modules:
  0.0 18.2 jit_solution(2993867266150188308)
XLA Ops:
  0.0 0.0 copy-start.4
  0.0 0.0 copy-start.2
  0.0 0.0 copy-start.3
  0.0 0.0 copy-start
  0.0 0.0 copy-start.1
  0.0 0.7 %copy-done.4 = s32[256]{0:T(256)S(1)} copy-done((s32[256]{0:T(256)S(1)}, s32[256]{0:T(256)}, u32[]{:S(2)}) %copy-start.4) | copy-done | bytes 1048
  0.7 0.0 copy-done.2
  0.7 0.0 copy-done.3
  0.7 0.0 copy-done
  0.7 0.0 copy-done.1
  0.7 0.7 %shard_map.64 = f32[32,8,128]{2,1,0:T(8,128)} custom-call(f32[2,256]{1,0:T(2,128)S(1)} %copy-done, s32[2,128]{1,0:T(2,128)S(1)} %bitcast.11, s32[2,128]{1,0:T(2,128)S(1)} %bitcast.12, s32[2,128]{1,0:T(2,128)S(1)} %bitcast.13, s32[2,128]{1,0:T(2,128)S(1)} %bitcast.14), custom_call_target="tpu_custom_call" | custom-call | tf_op jit(solution)/shard_map/pallas_call | solution.py:43
  1.4 7.3 %all-to-all-start = ((f32[32,8,128]{2,1,0:T(8,128)}), f32[32,8,128]{2,1,0:T(8,128)S(1)}, u32[]{:S(2)}, u32[]{:S(2)}) async-start(f32[32,8,128]{2,1,0:T(8,128)} %shard_map.64), calls=%async_computation | async-start | bytes 262144 | tf_op jit(solution)/shard_map/all_to_all | solution.py:218
  8.7 1.2 %copy.7 = bf16[8,256,128]{1,2,0:T(8,128)(2,1)S(1)} copy(bf16[8,256,128]{2,1,0:T(8,128)(2,1)} %bitcast.15) | data formatting | bytes 1048576 | tf_op jit(solution)/shard_map/reshape | solution.py:195
  10.0 6.2 %all-to-all-done = f32[32,8,128]{2,1,0:T(8,128)S(1)} async-done(((f32[32,8,128]{2,1,0:T(8,128)}), f32[32,8,128]{2,1,0:T(8,128)S(1)}, u32[]{:S(2)}, u32[]{:S(2)}) %all-to-all-start) | async-done | bytes 131104 | tf_op jit(solution)/shard_map/all_to_all | solution.py:218
  16.2 2.0 %shard_map.65 = f32[2,16,512]{2,1,0:T(8,128)} custom-call(f32[256,128]{1,0:T(8,128)S(1)} %bitcast.10, bf16[1024,256]{1,0:T(8,128)(2,1)S(1)} %bitcast.9), custom_call_target="tpu_custom_call" | custom-call | tf_op jit(solution)/shard_map/pallas_call | solution.py:203
Async XLA Ops:
  0.0 0.7 %copy-start.4 = (s32[256]{0:T(256)S(1)}, s32[256]{0:T(256)}, u32[]{:S(2)}) copy-start(s32[256]{0:T(256)} %param.11) | copy-start | bytes 3076
  0.0 0.7 %copy-start.2 = (s32[256,1]{0,1:T(1,128)S(1)}, s32[256,1]{0,1:T(1,128)}, u32[]{:S(2)}) copy-start(s32[256,1]{0,1:T(1,128)} %param.9) | copy-start | bytes 3076
  0.0 0.7 %copy-start.3 = (s32[256]{0:T(256)S(1)}, s32[256]{0:T(256)}, u32[]{:S(2)}) copy-start(s32[256]{0:T(256)} %param.10) | copy-start | bytes 3076
  0.0 0.7 %copy-start = (f32[2,256]{1,0:T(2,128)S(1)}, f32[2,256]{1,0:T(2,128)}, u32[]{:S(2)}) copy-start(f32[2,256]{1,0:T(2,128)} %vis_ref.1) | copy-start | bytes 6148
  0.0 0.7 %copy-start.1 = (s32[256]{0:T(256)S(1)}, s32[256]{0:T(256)}, u32[]{:S(2)}) copy-start(s32[256]{0:T(256)} %param.8) | copy-start | bytes 3076
  1.4 14.8 %all-to-all-start = ((f32[32,8,128]{2,1,0:T(8,128)}), f32[32,8,128]{2,1,0:T(8,128)S(1)}, u32[]{:S(2)}, u32[]{:S(2)}) async-start(f32[32,8,128]{2,1,0:T(8,128)} %shard_map.64), calls=%async_computation | async-start | bytes 262144 | tf_op jit(solution)/shard_map/all_to_all | solution.py:218

commit v3 on v2

--- a/solution.py
+++ b/solution.py
@@ -18,7 +18,14 @@
 PIECE = 256
 
 
-def pack_kernel(vis_ref, cell_ref, tile_ref, plane_ref, offset_ref, out_ref):
+def pack_kernel(*refs):
+    far, out_ref, near, sems = refs[:5], refs[6], refs[7:12], refs[12]
+    copies = [pltpu.make_async_copy(a, b, sems.at[i]) for i, (a, b) in enumerate(zip(far, near))]
+    for copy in copies:
+        copy.start()
+    for copy in copies:
+        copy.wait()
+    vis_ref, cell_ref, tile_ref, plane_ref, offset_ref = near
     rows = vis_ref.shape[1]
     address = (tile_ref[...] * (TILE_V * GRID_U) + cell_ref[...]).astype(jnp.float32)
     kind = (plane_ref[...] * (OVERSAMPLE * OVERSAMPLE) + offset_ref[...]).astype(jnp.float32)
@@ -37,16 +44,19 @@
         out_ref[d] = packed
 
 
-def pack(devices, visibility, cell, tile, plane, offset):
+def pack(devices, visibility, cell, tile, plane, offset, table):
     rows = visibility.shape[1]
     flat = [a.reshape(rows // LANES, LANES) for a in (cell, tile, plane, offset)]
+    operands = (visibility, *flat)
     return pl.pallas_call(
         pack_kernel,
         out_shape=jax.ShapeDtypeStruct((devices, rows // BLOCK * 8, LANES), jnp.float32),
-        in_specs=[pl.BlockSpec(memory_space=pltpu.VMEM)] * 5,
+        in_specs=[pl.BlockSpec(memory_space=pltpu.HBM)] * 6,
         out_specs=pl.BlockSpec(memory_space=pltpu.VMEM),
+        scratch_shapes=[pltpu.VMEM(a.shape, a.dtype) for a in operands]
+        + [pltpu.SemaphoreType.DMA((len(operands),))],
         compiler_params=pltpu.CompilerParams(vmem_limit_bytes=4 * 1024 * 1024),
-    )(visibility, *flat)
+    )(*[pltpu.with_memory_space_constraint(a, pltpu.HBM) for a in (*operands, table)])
 
 
 def along_lanes(values, index):
@@ -84,6 +94,8 @@
     first_u = lax.axis_index("chan") * width
     first_v = lax.axis_index("tile") * TILE_V
     sub = iota((8, LANES), 0)
+
+    turned_table = [table_ref[k : k + 256, :].T for k in range(0, table_ref.shape[0], 256)]
 
     def section(first_block, fresh):
         def column(q, first):
@@ -129,8 +141,8 @@
                 high = kind_n >> 8
                 onehot = jnp.where(iota((256, PIECE), 0) == low, 1.0, 0.0).astype(jnp.bfloat16)
                 kern = jnp.zeros((2 * AREA, PIECE), jnp.float32)
-                for t in range(table_ref.shape[0] // (2 * AREA)):
-                    part = dot(table_ref[t * 2 * AREA : (t + 1) * 2 * AREA, :], onehot, ((1,), (0,)))
+                for t in range(table_ref.shape[0] // 256):
+                    part = dot(turned_table[t], onehot, ((1,), (0,)))
                     kern = jnp.where(high == t, part, kern)
                 real_kern = kern[:AREA]
                 imag_kern = kern[AREA:]
@@ -191,8 +203,7 @@
 
 
 def table_of(kernel_table):
-    kernels = kernel_table.shape[0]
-    return kernel_table.reshape(kernels // 256, 256, 2 * AREA).transpose(0, 2, 1).reshape(-1, 256)
+    return kernel_table
 
 
 def grid(arrived, table, chans):
@@ -212,7 +223,7 @@
 
 def body(visibility, kernel_table, cell_index, tile_index, plane_index, offset_index):
     chans, tiles = lax.axis_size("chan"), lax.axis_size("tile")
-    packed = pack(chans * tiles, visibility, cell_index, tile_index[:, 0], plane_index, offset_index)
+    packed = pack(chans * tiles, visibility, cell_index, tile_index[:, 0], plane_index, offset_index, kernel_table)
     first = (chans - 1) // 2 * 2 * tiles + tiles - 1
     order = [first] + [c * tiles + t for t in range(tiles) for c in range(chans) if c * tiles + t != first]
     arrived = lax.all_to_all(

time: 18.6 us -> 17.8 us (0.957)
  blocking collectives: 0 us -> 14.6 us
  starting transfers between devices: 7.3 us -> 0 us
  waiting for transfers between devices: 6.23 us -> 0 us
  local copies, waits for them, and re-layouts: 1.98 us -> 0.01 us
  Pallas kernels: 2.68 us -> 2.88 us
    all_to_all x0 -> x1, blocking collectives: none -> 14.6 us  [body(): lax.all_to_all(packed, ('chan', 'tile'), split_axis=0, concat_axis=0, axi...]
    all_to_all x1 -> x0, starting transfers between devices: 7.3 us -> none  [body(): lax.all_to_all(packed, ('chan', 'tile'), split_axis=0, concat_axis=0, axi...]
    all_to_all x1 -> x0, waiting for transfers between devices: 6.23 us -> none  [body(): lax.all_to_all(packed, ('chan', 'tile'), split_axis=0, concat_axis=0, axi...]
    reshape x1 -> x0, local copies, waits for them, and re-layouts: 1.25 us -> none  [table_of(): kernel_table.reshape(kernels // 256, 256, 2 * AREA).transpose(0, 2, 1)]
    unnamed x10 -> x2, local copies, waits for them, and re-layouts: 0.73 us -> 0.01 us
    pallas_call x1, Pallas kernels: 0.66 us -> 0.86 us  [pack(): pl.pallas_call(pack_kernel, out_shape=jax.ShapeDtypeStruct((devices, rows...]
  transfers between devices with their start and end apart: 1 -> 0, of which waited for: 1 -> 0; matrix products, arithmetic and copies ran while one was open for 7% -> 0% of each run, Pallas kernels for 0% -> 0%
where the time goes in v3:
time: 17.8 us; the launch traced here: 17.5 us
  blocking collectives  14.6 us (82%)
  Pallas kernels  2.88 us (16%)
    all_to_all x1, blocking collectives, body(): lax.all_to_all(packed, ('chan', 'tile'), split_axis=0, concat_axis=0, axi...  14.6 us
    pallas_call x1, Pallas kernels, grid(): pl.pallas_call(functools.partial(grid_kernel, span), out_shape=jax.ShapeD...  2.02 us
    pallas_call x1, Pallas kernels, pack(): pl.pallas_call(pack_kernel, out_shape=jax.ShapeDtypeStruct((devices, rows...  0.86 us

profile of v3, /device:TPU:0, one launch (start us, length us, event | category | flops | bytes accessed | tf_op | source)
XLA Modules:
  0.0 17.5 jit_solution(2136203945427419449)
XLA Ops:
  0.0 0.0 copy-start
  0.0 0.9 %shard_map.64 = f32[32,8,128]{2,1,0:T(8,128)S(1)} custom-call(f32[2,256]{1,0:T(2,128)} %refs_0_.1, s32[2,128]{1,0:T(2,128)} %bitcast.6, s32[2,128]{1,0:T(2,128)} %bitcast.7, s32[2,128]{1,0:T(2,128)} %bitcast.8, s32[2,128]{1,0:T(2,128)} %bitcast.9, bf16[2048,128]{1,0:T(8,128)(2,1)} %table_ref.1), custom_call_target="tpu_custom_call" | custom-call | tf_op jit(solution)/shard_map/pallas_call | solution.py:51
  0.9 14.6 %all_to_all.5 = f32[32,8,128]{2,1,0:T(8,128)S(1)} all-to-all(f32[32,8,128]{2,1,0:T(8,128)S(1)} %shard_map.64), channel_id=1, replica_groups={{27,0,4,8,12,16,20,24,28,1,5,9,13,17,21,25,29,2,6,10,14,18,22,26,30,3,7..., dimensions={0} | all-to-all | bytes 262144 | tf_op jit(solution)/shard_map/all_to_all | solution.py:229
  15.5 0.0 copy-done
  15.5 2.0 %shard_map.65 = f32[2,16,512]{2,1,0:T(8,128)} custom-call(f32[256,128]{1,0:T(8,128)S(1)} %bitcast.5, bf16[2048,128]{1,0:T(8,128)(2,1)S(1)} %copy-done), custom_call_target="tpu_custom_call" | custom-call | tf_op jit(solution)/shard_map/pallas_call | solution.py:214
Async XLA Ops:
  0.0 15.5 %copy-start = (bf16[2048,128]{1,0:T(8,128)(2,1)S(1)}, bf16[2048,128]{1,0:T(8,128)(2,1)}, u32[]{:S(2)}) copy-start(bf16[2048,128]{1,0:T(8,128)(2,1)} %table_ref.1) | copy-start | bytes 1572868

commit v4 on v3

--- a/solution.py
+++ b/solution.py
@@ -1,4 +1,5 @@
 import functools
+import itertools
 
 import jax
 import jax.numpy as jnp
@@ -88,9 +89,9 @@
     return ranks, above
 
 
-def grid_kernel(span, rows_ref, table_ref, out_ref, total_ref):
+def grid_kernel(span, own_ref, other_ref, table_ref, out_ref, total_ref):
     width = out_ref.shape[2]
-    blocks = rows_ref.shape[0] // 8
+    blocks = own_ref.shape[0] // 8
     first_u = lax.axis_index("chan") * width
     first_v = lax.axis_index("tile") * TILE_V
     sub = iota((8, LANES), 0)
@@ -98,21 +99,20 @@
     turned_table = [table_ref[k : k + 256, :].T for k in range(0, table_ref.shape[0], 256)]
 
     def section(first_block, fresh):
-        def column(q, first):
-            return rows_ref[pl.ds(first_block * 8 + first * 8 + q, 8, stride=8), :]
+        def column(ref, q, first):
+            return ref[pl.ds(first_block * 8 + first * 8 + q, 8, stride=8), :]
 
         real, imag, code, marks = [], [], [], []
-        for half in range(2):
-            for first in range(0, span, 8):
-                real.append(column(half, first))
-                imag.append(column(2 + half, first))
-                address = column(4 + half, first).astype(jnp.int32)
-                kind = column(6 + half, first).astype(jnp.int32)
-                v_rel = (address >> 12) - first_v
-                u_rel = (address & (GRID_U - 1)) - first_u
-                touches = (v_rel > -SUPPORT) & (v_rel < TILE_V) & (u_rel > -SUPPORT) & (u_rel < width)
-                marks.append(jnp.where(touches, 1, 0))
-                code.append(kind + ((u_rel + SUPPORT) << 11) + ((v_rel + SUPPORT) << 24))
+        for ref, half, first in itertools.product((own_ref, other_ref), range(2), range(0, span, 8)):
+            real.append(column(ref, half, first))
+            imag.append(column(ref, 2 + half, first))
+            address = column(ref, 4 + half, first).astype(jnp.int32)
+            kind = column(ref, 6 + half, first).astype(jnp.int32)
+            v_rel = (address >> 12) - first_v
+            u_rel = (address & (GRID_U - 1)) - first_u
+            touches = (v_rel > -SUPPORT) & (v_rel < TILE_V) & (u_rel > -SUPPORT) & (u_rel < width)
+            marks.append(jnp.where(touches, 1, 0))
+            code.append(kind + ((u_rel + SUPPORT) << 11) + ((v_rel + SUPPORT) << 24))
         ranks, total = ranks_down(marks)
         ranks = [jnp.where(m > 0, r, -1) for m, r in zip(marks, ranks)]
         lines = [[jnp.broadcast_to(r[j : j + 1], r.shape) for j in range(8)] for r in ranks]
@@ -207,29 +207,30 @@
 
 
 def grid(arrived, table, chans):
-    rows = arrived.reshape(-1, LANES)
-    blocks = rows.shape[0] // 8
-    span = 32 if blocks % 32 == 0 else blocks
+    rows = [part.reshape(-1, LANES) for part in arrived]
+    blocks = rows[0].shape[0] // 8
+    span = 16 if blocks % 16 == 0 else blocks
     width = GRID_U // chans
     return pl.pallas_call(
         functools.partial(grid_kernel, span),
         out_shape=jax.ShapeDtypeStruct((2, TILE_V, width), jnp.float32),
-        in_specs=[pl.BlockSpec(memory_space=pltpu.VMEM)] * 2,
+        in_specs=[pl.BlockSpec(memory_space=pltpu.VMEM)] * 3,
         out_specs=pl.BlockSpec(memory_space=pltpu.VMEM),
         scratch_shapes=[pltpu.VMEM((2 * TILE_V * SUPPORT, width), jnp.float32)],
         compiler_params=pltpu.CompilerParams(vmem_limit_bytes=32 * 1024 * 1024),
-    )(rows, table)
+    )(*rows, table)
 
 
 def body(visibility, kernel_table, cell_index, tile_index, plane_index, offset_index):
     chans, tiles = lax.axis_size("chan"), lax.axis_size("tile")
-    packed = pack(chans * tiles, visibility, cell_index, tile_index[:, 0], plane_index, offset_index, kernel_table)
-    first = (chans - 1) // 2 * 2 * tiles + tiles - 1
-    order = [first] + [c * tiles + t for t in range(tiles) for c in range(chans) if c * tiles + t != first]
+    packed = pack(chans // 2 * tiles, visibility, cell_index, tile_index[:, 0], plane_index, offset_index, kernel_table)
+    chips = [(c, t) for t in range(tiles) for c in range(0, chans, 2)][::-1]
+    groups = [[(c + (side ^ (2 * t >= tiles))) * tiles + t for c, t in chips] for side in range(2)]
     arrived = lax.all_to_all(
-        packed, ("chan", "tile"), split_axis=0, concat_axis=0, axis_index_groups=[order]
+        packed, ("chan", "tile"), split_axis=0, concat_axis=0, axis_index_groups=groups
     )
-    return grid(arrived, table_of(kernel_table), chans)
+    swapped = lax.ppermute(arrived, "chan", [(c, c ^ 1) for c in range(chans)])
+    return grid((arrived, swapped), table_of(kernel_table), chans)
 
 
 def solution(mesh):

time: 17.8 us -> 16.2 us (0.910)
  blocking collectives: 14.6 us -> 11.6 us
  waiting for transfers between devices: 0 us -> 0.9 us
  starting transfers between devices: 0 us -> 0.59 us
    all_to_all x1, blocking collectives: 14.6 us -> 11.6 us  [body(): lax.all_to_all(packed, ('chan', 'tile'), split_axis=0, concat_axis=0, axi...]
    ppermute x0 -> x1, waiting for transfers between devices: none -> 0.9 us  [body(): swapped = lax.ppermute(arrived, 'chan', [(c, c ^ 1) for c in range(chans)])]
    ppermute x0 -> x1, starting transfers between devices: none -> 0.59 us  [body(): swapped = lax.ppermute(arrived, 'chan', [(c, c ^ 1) for c in range(chans)])]
  transfers between devices with their start and end apart: 0 -> 1, of which waited for: 0 -> 1; matrix products, arithmetic and copies ran while one was open for 0% -> 0% of each run, Pallas kernels for 0% -> 0%
where the time goes in v4:
time: 16.2 us; the launch traced here: 15.9 us
  blocking collectives  11.6 us (72%)
  Pallas kernels  2.88 us (18%)
  waiting for transfers between devices  0.9 us (6%)
  starting transfers between devices  0.59 us (4%)
    all_to_all x1, blocking collectives, body(): lax.all_to_all(packed, ('chan', 'tile'), split_axis=0, concat_axis=0, axi...  11.6 us
    pallas_call x1, Pallas kernels, grid(): pl.pallas_call(functools.partial(grid_kernel, span), out_shape=jax.ShapeD...  2.02 us
    ppermute x1, waiting for transfers between devices, body(): swapped = lax.ppermute(arrived, 'chan', [(c, c ^ 1) for c in range(chans)])  0.9 us
    pallas_call x1, Pallas kernels, pack(): pl.pallas_call(pack_kernel, out_shape=jax.ShapeDtypeStruct((devices, rows...  0.85 us
    ppermute x1, starting transfers between devices, body(): swapped = lax.ppermute(arrived, 'chan', [(c, c ^ 1) for c in range(chans)])  0.59 us
  transfers between devices with their start and end apart: 1, of which 1 were waited for; matrix products, arithmetic and copies ran while one was open for 0% of the time, Pallas kernels for 0%

profile of v4, /device:TPU:0, one launch (start us, length us, event | category | flops | bytes accessed | tf_op | source)
XLA Modules:
  0.0 15.9 jit_solution(14349308919496287712)
XLA Ops:
  0.0 0.0 copy-start
  0.0 0.9 %shard_map.64 = f32[16,8,128]{2,1,0:T(8,128)S(1)} custom-call(f32[2,256]{1,0:T(2,128)} %refs_0_.1, s32[2,128]{1,0:T(2,128)} %bitcast.8, s32[2,128]{1,0:T(2,128)} %bitcast.9, s32[2,128]{1,0:T(2,128)} %bitcast.10, s32[2,128]{1,0:T(2,128)} %bitcast.11, bf16[2048,128]{1,0:T(8,128)(2,1)} %table_ref.1), custom_call_target="tpu_custom_call" | custom-call | tf_op jit(solution)/shard_map/pallas_call | solution.py:52
  0.9 11.6 %all_to_all.5 = f32[16,8,128]{2,1,0:T(8,128)S(1)} all-to-all(f32[16,8,128]{2,1,0:T(8,128)S(1)} %shard_map.64), channel_id=1, replica_groups={{31,23,15,7,30,22,14,6,25,17,9,1,24,16,8,0},{27,19,11,3,26,18,10,2,29,2..., dimensions={0} | all-to-all | bytes 131072 | tf_op jit(solution)/shard_map/all_to_all | solution.py:229
  12.4 0.6 %collective-permute-start = (f32[16,8,128]{2,1,0:T(8,128)S(1)}, f32[16,8,128]{2,1,0:T(8,128)S(1)}, u32[]{:S(2)}, u32[]{:S(2)}) collective-permute-start(f32[16,8,128]{2,1,0:T(8,128)S(1)} %all_to_all.5), channel_id=1, source_target_pairs={{0,4},{4,0},{8,12},{12,8},{16,20},{20,16},{24,28},{28,24},{1,5},{5... | collective-permute-start | bytes 196616 | tf_op jit(solution)/shard_map/ppermute | solution.py:232
  13.0 0.9 %collective-permute-done = f32[16,8,128]{2,1,0:T(8,128)S(1)} collective-permute-done((f32[16,8,128]{2,1,0:T(8,128)S(1)}, f32[16,8,128]{2,1,0:T(8,128)S(1)}, u32[]{:S(2)}, u32[]{:S(2)}) %collective-permute-start) | collective-permute-done | bytes 65568 | tf_op jit(solution)/shard_map/ppermute | solution.py:232
  13.9 0.0 copy-done
  13.9 2.0 %shard_map.65 = f32[2,16,512]{2,1,0:T(8,128)} custom-call(f32[128,128]{1,0:T(8,128)S(1)} %bitcast.6, f32[128,128]{1,0:T(8,128)S(1)} %bitcast.7, bf16[2048,128]{1,0:T(8,128)(2,1)S(1)} %copy-done), custom_call_target="tpu_custom_call" | custom-call | tf_op jit(solution)/shard_map/pallas_call | solution.py:214
Async XLA Ops:
  0.0 13.9 %copy-start = (bf16[2048,128]{1,0:T(8,128)(2,1)S(1)}, bf16[2048,128]{1,0:T(8,128)(2,1)}, u32[]{:S(2)}) copy-start(bf16[2048,128]{1,0:T(8,128)(2,1)} %table_ref.1) | copy-start | bytes 1572868
  12.4 1.5 %collective-permute-start = (f32[16,8,128]{2,1,0:T(8,128)S(1)}, f32[16,8,128]{2,1,0:T(8,128)S(1)}, u32[]{:S(2)}, u32[]{:S(2)}) collective-permute-start(f32[16,8,128]{2,1,0:T(8,128)S(1)} %all_to_all.5), channel_id=1, source_target_pairs={{0,4},{4,0},{8,12},{12,8},{16,20},{20,16},{24,28},{28,24},{1,5},{5... | collective-permute-start | bytes 196616 | tf_op jit(solution)/shard_map/ppermute | solution.py:232

commit v5 on v4

v5 whole, which is shorter than its diff:
```python
import functools

import jax
import jax.numpy as jnp
from jax import lax
from jax.experimental import pallas as pl
from jax.experimental.pallas import tpu as pltpu
from jax.sharding import PartitionSpec as P

GRID_U = 4096
SUPPORT = 8
OVERSAMPLE = 8
TILE_V = 16
AREA = SUPPORT * SUPPORT
LANES = 128
BLOCK = 2 * LANES
PLAIN = 1
DEEP = 6
FIRST_SHARE = 16
SECOND_SHARE = 32
PIECE = 256


def pack_kernel(*refs):
    far, out_ref, near, sems = refs[:5], refs[6], refs[7:12], refs[12]
    copies = [pltpu.make_async_copy(a, b, sems.at[i]) for i, (a, b) in enumerate(zip(far, near))]
    for copy in copies:
        copy.start()
    for copy in copies:
        copy.wait()
    vis_ref, cell_ref, tile_ref, plane_ref, offset_ref = near
    rows = vis_ref.shape[1]
    address = (tile_ref[...] * (TILE_V * GRID_U) + cell_ref[...]).astype(jnp.float32)
    kind = (plane_ref[...] * (OVERSAMPLE * OVERSAMPLE) + offset_ref[...]).astype(jnp.float32)
    parts = []
    for first in range(0, rows, BLOCK):
        for q in range(2):
            for half in range(2):
                start = first + half * LANES
                parts.append(vis_ref[q : q + 1, start : start + LANES])
        at = first // LANES
        parts.append(address[at : at + 2])
        parts.append(kind[at : at + 2])
    packed = jnp.concatenate(parts, axis=0)

    for d in range(out_ref.shape[0]):
        out_ref[d] = packed


def pack(devices, visibility, cell, tile, plane, offset, table):
    rows = visibility.shape[1]
    flat = [a.reshape(rows // LANES, LANES) for a in (cell, tile, plane, offset)]
    operands = (visibility, *flat)
    return pl.pallas_call(
        pack_kernel,
        out_shape=jax.ShapeDtypeStruct((devices, rows // BLOCK * 8, LANES), jnp.float32),
        in_specs=[pl.BlockSpec(memory_space=pltpu.HBM)] * 6,
        out_specs=pl.BlockSpec(memory_space=pltpu.VMEM),
        scratch_shapes=[pltpu.VMEM(a.shape, a.dtype) for a in operands]
        + [pltpu.SemaphoreType.DMA((len(operands),))],
        compiler_params=pltpu.CompilerParams(vmem_limit_bytes=4 * 1024 * 1024),
    )(*[pltpu.with_memory_space_constraint(a, pltpu.HBM) for a in (*operands, table)])


def along_lanes(values, index):
    return jnp.take_along_axis(values, index, axis=1, mode="promise_in_bounds")


def along_sublanes(values, index):
    return jnp.take_along_axis(values, index, axis=0, mode="promise_in_bounds")


def iota(shape, axis):
    return lax.broadcasted_iota(jnp.int32, shape, axis)


def dot(a, b, dims):
    return lax.dot_general(a, b, (dims, ((), ())), preferred_element_type=jnp.float32)


class Gridder:
    def __init__(self, width, table_ref):
        self.width = width
        self.first_u = lax.axis_index("chan") * width
        self.first_v = lax.axis_index("tile") * TILE_V
        self.half = iota((8, LANES), 0) & 1
        self.rows_b = iota((256, PIECE), 0).astype(jnp.float32).astype(jnp.bfloat16)
        self.table = [table_ref[k : k + 256, :].T for k in range(0, table_ref.shape[0], 256)]

    def line(self, values):
        return jnp.broadcast_to(values.astype(jnp.float32).astype(jnp.bfloat16), (256, PIECE))

    def sums(self, tiles):
        width, one, zero = self.width, jnp.bfloat16(1), jnp.bfloat16(0)
        spreads, places = [], []
        for tile in tiles:
            vr, vi, address, kind = [
                jnp.concatenate([tile[2 * q : 2 * q + 1], tile[2 * q + 1 : 2 * q + 2]], axis=1) for q in range(4)
            ]
            address = address.astype(jnp.int32)
            kind = kind.astype(jnp.int32)
            u_n = (address & (GRID_U - 1)) - self.first_u
            v_n = (address >> 12) - self.first_v
            high = kind >> 8
            onehot = jnp.where(self.rows_b == self.line(kind & 255), one, zero)
            kern = jnp.zeros((2 * AREA, PIECE), jnp.float32)
            for k, part in enumerate(self.table):
                kern = jnp.where(high == k, dot(part, onehot, ((1,), (0,))), kern)
            real_kern = kern[:AREA]
            imag_kern = kern[AREA:]
            weighted = (vr * real_kern - vi * imag_kern, vr * imag_kern + vi * real_kern)
            sub = iota((SUPPORT, PIECE), 0)
            turn = (sub - v_n) & (SUPPORT - 1)
            inside = [(sub + 8 * y >= v_n) & (sub + 8 * y < v_n + SUPPORT) for y in range(2)]
            spread = []
            for i in range(SUPPORT):
                in_u = (u_n + i >= 0) & (u_n + i < width)
                for c in range(2):
                    turned = along_sublanes(weighted[c][i * 8 : (i + 1) * 8], turn)
                    for y in range(2):
                        spread.append(jnp.where(inside[y] & in_u, turned, 0.0))
            spreads.append(jnp.concatenate(spread, axis=0).astype(jnp.bfloat16))
            column = jnp.where(u_n < 0, u_n + width, u_n)
            near = jnp.where(self.rows_b == self.line(column & 255), one, zero)
            far = self.line(column >> 8)
            place = [jnp.where(far == h, near, zero) for h in range(-(-width // 256))]
            places.append(jnp.concatenate(place, axis=0)[:width])
        return dot(jnp.concatenate(spreads, axis=1), jnp.concatenate(places, axis=1), ((1,), (1,)))

    def marked(self, rows_ref, first_block, span):
        tiles, ranks = [], []
        total = jnp.zeros((8, LANES), jnp.int32)
        for block in range(span):
            tile = rows_ref[pl.ds((first_block + block) * 8, 8), :]
            address = tile.astype(jnp.int32)
            v_rel = (address >> 12) - self.first_v
            u_rel = (address & (GRID_U - 1)) - self.first_u
            touches = (v_rel > -SUPPORT) & (v_rel < TILE_V) & (u_rel > -SUPPORT) & (u_rel < self.width)
            here = along_sublanes(jnp.where(touches, 1, 0), 4 + self.half)
            ranks.append(jnp.where(here > 0, total, -1))
            tiles.append(tile)
            total = total + here
        return tiles, ranks, total

    def later_sections(self, rows_ref, span, sums_ref):
        blocks = rows_ref.shape[0] // 8
        if blocks > span:

            @pl.loop(1, blocks // span)
            def _(section):
                tiles, ranks, total = self.marked(rows_ref, section * span, span)

                @pl.loop(0, (jnp.max(total) + 1) // 2)
                def _(pair):
                    sums_ref[...] += self.sums([ranked(tiles, ranks, 2 * pair + e) for e in range(2)])


def ranked(tiles, ranks, wanted):
    got = jnp.zeros((8, LANES), jnp.float32)
    for tile, rank in zip(tiles, ranks):
        got = jnp.where(rank == wanted, tile, got)
    return got


def add_rows(grid, share, span, rows_ref, sums_ref, first):
    sub, lane = iota((8, LANES), 0), iota((8, LANES), 1)
    half = grid.half
    tiles, ranks, total = grid.marked(rows_ref, 0, span)
    beyond = jnp.maximum(total - PLAIN, 0)
    skip = jnp.zeros_like(beyond)
    every = beyond
    for by in range(share, LANES, share):
        earlier = pltpu.roll(beyond, by, axis=1)
        skip = skip + jnp.where(lane >= by, earlier, 0)
        every = every + earlier
    skip = skip + jnp.where(half > 0, along_sublanes(every, sub ^ 1), 0)
    plain = [ranked(tiles, ranks, r) for r in range(PLAIN)]
    more = [ranked(tiles, ranks, r) for r in range(PLAIN, DEEP)]
    slots = 2 * LANES // share
    moved = []
    for slot in range(slots):
        got = jnp.zeros((8, LANES), jnp.float32)
        for k, tile in enumerate(more):
            got = jnp.where(skip == slot - k, tile, got)
        moved.append(got)
    folded = []
    for even, odd in zip(moved[::2], moved[1::2]):
        folded.append(jnp.where(half == 0, even, odd) + along_sublanes(jnp.where(half == 0, odd, even), sub ^ 1))
    by = LANES // 2
    while by >= share:
        count = len(folded) // 2
        upper = (lane & by) > 0
        folded = [
            jnp.where(upper, folded[k + count], folded[k])
            + along_lanes(jnp.where(upper, folded[k], folded[k + count]), lane ^ by)
            for k in range(count)
        ]
        by //= 2
    sums_ref[...] = first(grid.sums([*plain, *folded]))
    done = jnp.clip(PLAIN + slots - skip, PLAIN, DEEP)

    @pl.loop(0, (jnp.max(total - done) + 1) // 2)
    def _(pair):
        sums_ref[...] += grid.sums([ranked(tiles, ranks, done + (2 * pair + e)) for e in range(2)])

    grid.later_sections(rows_ref, span, sums_ref)


def first_kernel(span, rows_ref, table_ref, sums_ref):
    add_rows(Gridder(sums_ref.shape[1], table_ref), FIRST_SHARE, span, rows_ref, sums_ref, lambda sums: sums)


def second_kernel(span, rows_ref, table_ref, begun_ref, out_ref, sums_ref):
    grid = Gridder(out_ref.shape[2], table_ref)
    add_rows(grid, SECOND_SHARE, span, rows_ref, sums_ref, lambda sums: begun_ref[...] + sums)
    both = 2 * TILE_V
    result = sums_ref[0:both, :]
    for i in range(1, SUPPORT):
        result = result + pltpu.roll(sums_ref[i * both : (i + 1) * both, :], i, axis=1)
    out_ref[0] = result[:TILE_V]
    out_ref[1] = result[TILE_V:]


def grid(own, other, table, chans):
    own, other = [part.reshape(-1, LANES) for part in (own, other)]
    blocks = own.shape[0] // 8
    span = 16 if blocks % 16 == 0 else blocks
    width = GRID_U // chans
    taps = 2 * TILE_V * SUPPORT
    vmem = pl.BlockSpec(memory_space=pltpu.VMEM)
    params = pltpu.CompilerParams(vmem_limit_bytes=16 * 1024 * 1024)
    cost = pl.CostEstimate(flops=10**9, bytes_accessed=10**6, transcendentals=0)
    begun = pl.pallas_call(
        functools.partial(first_kernel, span),
        out_shape=pltpu.VMEM((taps, width), jnp.float32),
        in_specs=[vmem] * 2,
        out_specs=vmem,
        compiler_params=params,
        cost_estimate=cost,
    )(own, table)
    return pl.pallas_call(
        functools.partial(second_kernel, span),
        out_shape=jax.ShapeDtypeStruct((2, TILE_V, width), jnp.float32),
        in_specs=[vmem] * 3,
        out_specs=vmem,
        scratch_shapes=[pltpu.VMEM((taps, width), jnp.float32)],
        compiler_params=params,
        cost_estimate=cost,
    )(other, table, begun)


def body(visibility, kernel_table, cell_index, tile_index, plane_index, offset_index):
    chans, tiles = lax.axis_size("chan"), lax.axis_size("tile")
    packed = pack(chans // 2 * tiles, visibility, cell_index, tile_index[:, 0], plane_index, offset_index, kernel_table)
    chips = [(c, t) for t in range(tiles) for c in range(0, chans, 2)][::-1]
    chips.insert(0, chips.pop(chans // 2))
    groups = [[(c + (side ^ (4 * t >= 3 * tiles))) * tiles + t for c, t in chips] for side in range(2)]
    arrived = lax.all_to_all(
        packed, ("chan", "tile"), split_axis=0, concat_axis=0, axis_index_groups=groups
    )
    swapped = lax.ppermute(arrived, "chan", [(c, c ^ 1) for c in range(chans)])
    return grid(arrived, swapped, kernel_table, chans)


def solution(mesh):
    placed = (
        P(None, ("chan", "tile")),
        P(),
        P(("chan", "tile")),
        P(("chan", "tile"), None),
        P(("chan", "tile")),
        P(("chan", "tile")),
    )
    return jax.shard_map(
        body, mesh=mesh, in_specs=placed, out_specs=P(None, "tile", "chan"), check_vma=False
    )
```

time: 16.2 us -> 15.5 us (0.957)
  waiting for transfers between devices: 0.9 us -> 0.01 us
  Pallas kernels: 2.88 us -> 3.46 us
  starting transfers between devices: 0.59 us -> 0.35 us
    ppermute x1, waiting for transfers between devices: 0.9 us -> 0.01 us  [body(): swapped = lax.ppermute(arrived, 'chan', [(c, c ^ 1) for c in range(chans)])]
    pallas_call x1 -> x2, Pallas kernels: 2.02 us -> 2.6 us  [the longest x1 1.69 us: grid(): pl.pallas_call(functools.partial(second_kernel, span), out_shape=jax.Shap...]
    ppermute x1, starting transfers between devices: 0.59 us -> 0.35 us  [body(): swapped = lax.ppermute(arrived, 'chan', [(c, c ^ 1) for c in range(chans)])]
  transfers between devices with their start and end apart: 1 -> 1, of which waited for: 1 -> 0; matrix products, arithmetic and copies ran while one was open for 0% -> 0% of each run, Pallas kernels for 0% -> 6%
where the time goes in v5:
time: 15.5 us; the launch traced here: 15.3 us
  blocking collectives  11.5 us (74%)
  Pallas kernels  3.46 us (22%)
  starting transfers between devices  0.35 us (2%)
    all_to_all x1, blocking collectives, body(): lax.all_to_all(packed, ('chan', 'tile'), split_axis=0, concat_axis=0, axi...  11.5 us
    pallas_call x1, Pallas kernels, grid(): pl.pallas_call(functools.partial(second_kernel, span), out_shape=jax.Shap...  1.69 us
    pallas_call x1, Pallas kernels, grid(): pl.pallas_call(functools.partial(first_kernel, span), out_shape=pltpu.VME...  0.92 us
    pallas_call x1, Pallas kernels, pack(): pl.pallas_call(pack_kernel, out_shape=jax.ShapeDtypeStruct((devices, rows...  0.85 us
    ppermute x1, starting transfers between devices, body(): swapped = lax.ppermute(arrived, 'chan', [(c, c ^ 1) for c in range(chans)])  0.35 us
  transfers between devices with their start and end apart: 1, of which 0 were waited for; matrix products, arithmetic and copies ran while one was open for 0% of the time, Pallas kernels for 6%

profile of v5, /device:TPU:0, one launch (start us, length us, event | category | flops | bytes accessed | tf_op | source)
XLA Modules:
  0.0 15.3 jit_solution(14049227393876087966)
XLA Ops:
  0.0 0.0 copy-start
  0.0 0.9 %shard_map.64 = f32[16,8,128]{2,1,0:T(8,128)S(1)} custom-call(f32[2,256]{1,0:T(2,128)} %refs_0_.1, s32[2,128]{1,0:T(2,128)} %bitcast.8, s32[2,128]{1,0:T(2,128)} %bitcast.9, s32[2,128]{1,0:T(2,128)} %bitcast.10, s32[2,128]{1,0:T(2,128)} %bitcast.11, bf16[2048,128]{1,0:T(8,128)(2,1)} %table_ref.3), custom_call_target="tpu_custom_call" | custom-call | tf_op jit(solution)/shard_map/pallas_call | solution.py:54
  0.9 11.5 %all_to_all.5 = f32[16,8,128]{2,1,0:T(8,128)S(1)} all-to-all(f32[16,8,128]{2,1,0:T(8,128)S(1)} %shard_map.64), channel_id=1, replica_groups={{26,31,23,15,7,18,10,2,25,17,9,1,24,16,8,0},{30,27,19,11,3,22,14,6,29,2..., dimensions={0} | all-to-all | bytes 131072 | tf_op jit(solution)/shard_map/all_to_all | solution.py:258
  12.4 0.4 %collective-permute-start = (f32[16,8,128]{2,1,0:T(8,128)S(1)}, f32[16,8,128]{2,1,0:T(8,128)S(1)}, u32[]{:S(2)}, u32[]{:S(2)}) collective-permute-start(f32[16,8,128]{2,1,0:T(8,128)S(1)} %all_to_all.5), channel_id=1, source_target_pairs={{0,4},{4,0},{8,12},{12,8},{16,20},{20,16},{24,28},{28,24},{1,5},{5... | collective-permute-start | bytes 196616 | tf_op jit(solution)/shard_map/ppermute | solution.py:261
  12.7 0.0 copy-done
  12.7 0.9 %shard_map.65.begun_ref = f32[256,512]{1,0:T(8,128)S(1)} custom-call(f32[128,128]{1,0:T(8,128)S(1)} %bitcast.6, bf16[2048,128]{1,0:T(8,128)(2,1)S(1)} %copy-done), custom_call_target="tpu_custom_call" | custom-call | flops 1000000000 | bytes 1000000 | tf_op jit(solution)/shard_map/pallas_call | solution.py:233
  13.6 0.0 collective-permute-done
  13.7 1.7 %shard_map.66 = f32[2,16,512]{2,1,0:T(8,128)} custom-call(f32[128,128]{1,0:T(8,128)S(1)} %bitcast.7, bf16[2048,128]{1,0:T(8,128)(2,1)S(1)} %copy-done, f32[256,512]{1,0:T(8,128)S(1)} %shard_map.65.begun_ref), custom_call_target="tpu_custom_call" | custom-call | flops 1000000000 | bytes 1000000 | tf_op jit(solution)/shard_map/pallas_call | solution.py:241
Async XLA Ops:
  0.0 12.7 %copy-start = (bf16[2048,128]{1,0:T(8,128)(2,1)S(1)}, bf16[2048,128]{1,0:T(8,128)(2,1)}, u32[]{:S(2)}) copy-start(bf16[2048,128]{1,0:T(8,128)(2,1)} %table_ref.3) | copy-start | bytes 1572868
  12.4 1.3 %collective-permute-start = (f32[16,8,128]{2,1,0:T(8,128)S(1)}, f32[16,8,128]{2,1,0:T(8,128)S(1)}, u32[]{:S(2)}, u32[]{:S(2)}) collective-permute-start(f32[16,8,128]{2,1,0:T(8,128)S(1)} %all_to_all.5), channel_id=1, source_target_pairs={{0,4},{4,0},{8,12},{12,8},{16,20},{20,16},{24,28},{28,24},{1,5},{5... | collective-permute-start | bytes 196616 | tf_op jit(solution)/shard_map/ppermute | solution.py:261
